TPU v7x, 128 devices: a whole 4x4x4 slice. The times are simulated.
128 devices in a mesh: section: 16 (over x_lo, z, core), dp: 8 (over y, x_hi).
Axes of the slice: x: 4 (x_hi: 2, x_lo: 2; x = x_hi * 2 + x_lo), y: 4, z: 4, core: 2. Of those that a mesh axis runs over, the one named last changes fastest.
Arguments:
- in_bases: bfloat16 [16, 8, 10, 24, 8192], P('section', 'dp'), may hold values from -6 to 6
- sent_bases: bfloat16 [16, 8, 10, 24, 8192], P('section', 'dp'), may hold values from -6 to 6
- sample_ids: int32 [8, 8], P('dp'), may hold values from 0 to 9
- exponents: int32 [8, 8, 24, 64], P('dp'), may hold values from -8 to -5
- cotangent: bfloat16 [8, 8, 24, 8192], P('dp'), may hold values from -6 to 6
- w_down: bfloat16 [16, 8192, 256], P('section'), may hold values from -0.0625 to 0.0625
- w_up: bfloat16 [16, 256, 8192], P('section'), may hold values from -0.375 to 0.375
- norm_gain: float32 [16, 8192], P('section'), may hold values from 0.5 to 1.5
Outputs:
- rebuilt: bfloat16 [16, 8, 8, 24, 8192], P('section', 'dp')
- grad_down: float32 [16, 8192, 256], P('section', 'dp')
- grad_up: float32 [16, 256, 8192], P('section', None, 'dp')
- gain_grad: float32 [16, 8192], P('section', 'dp')
All inputs are finite; a program needn't handle non-finite values.
Results may differ from a plain program's by a relative error of at most 0.03.
Values may be sent and summed in bfloat16 or wider, within the bound.
A program may use at most 128 MiB of HBM per device.

v0:
```python
import jax
import jax.numpy as jnp
from jax import lax
from jax.sharding import PartitionSpec as P

D = 8192
BLOCK = 128


LIMIT = 448.0
EPSILON = 1e-05


def from_behind(value, axis, steps):
    count = lax.axis_size(axis)
    initial, last = (max(0, -steps), min(count, count - steps))
    return lax.ppermute(value, axis, [(source, source + steps) for source in range(initial, last)])


def normalize(inputs):
    widened = inputs.astype(jnp.float32)
    spread = jnp.sqrt(jnp.mean(widened * widened, axis=-1, keepdims=True) + EPSILON)
    return (widened / spread, spread)


def dequantize(delta_codes, block_exps):
    shaped = delta_codes.astype(jnp.float32).reshape(delta_codes.shape[:-1] + (D // BLOCK, BLOCK))
    factor = jnp.exp2(block_exps.astype(jnp.float32))[..., None]
    return (shaped * factor).reshape(delta_codes.shape)


def quantize(difference, block_exps):
    shaped = difference.reshape(difference.shape[:-1] + (D // BLOCK, BLOCK))
    factor = jnp.exp2(-block_exps.astype(jnp.float32))[..., None]
    return jnp.clip(shaped * factor, -LIMIT, LIMIT).reshape(difference.shape).astype(jnp.bfloat16)


def layer_forward(inputs, down_proj, up_proj, scale_gain):
    normed, spread = normalize(inputs)
    hidden = (normed * scale_gain).astype(jnp.bfloat16)
    inner = jnp.dot(hidden, down_proj, preferred_element_type=jnp.float32)
    active = jax.nn.silu(inner).astype(jnp.bfloat16)
    output = inputs.astype(jnp.float32) + jnp.dot(
        active, up_proj, preferred_element_type=jnp.float32
    )
    return (hidden, inner, active, output)


def layer_backward(grad_out, normed, spread, inner, down_proj, up_proj, scale_gain):
    grad_active = lax.dot_general(
        grad_out, up_proj, (((1,), (1,)), ((), ())), preferred_element_type=jnp.float32
    )
    sigma = jax.nn.sigmoid(inner)
    grad_inner = (grad_active * sigma * (1.0 + inner * (1.0 - sigma))).astype(jnp.bfloat16)
    grad_hidden = lax.dot_general(
        grad_inner, down_proj, (((1,), (1,)), ((), ())), preferred_element_type=jnp.float32
    )
    gain_terms = jnp.sum(grad_hidden * normed, axis=0)
    grad_normed = grad_hidden * scale_gain
    grad_input = (
        grad_out.astype(jnp.float32)
        + (grad_normed - normed * jnp.mean(grad_normed * normed, axis=-1, keepdims=True)) / spread
    )
    return (grad_input.astype(jnp.bfloat16), grad_inner, gain_terms)


def pick(stored_table, position_now):
    return lax.dynamic_index_in_dim(stored_table, position_now, 0, keepdims=False)


def keep_slot(buffer, new_value, position_now, live_tick):
    previous = pick(buffer, position_now)
    chosen = jnp.where(live_tick, new_value, previous)
    return lax.dynamic_update_index_in_dim(buffer, chosen, position_now, 0)


def contract_rows(left_side, right_side):
    return lax.dot_general(
        left_side, right_side, (((0,), (0,)), ((), ())), preferred_element_type=jnp.float32
    )


def on_device(in_bases, sent_bases, sample_ids, exponents, cotangent, w_down, w_up, norm_gain):
    sections = lax.axis_size("section")
    my_section = lax.axis_index("section")
    micro_count = sample_ids.shape[1]
    row_count = in_bases.shape[3]
    feature_count = in_bases.shape[4]
    adapter = w_down.shape[2]
    table_in = in_bases[0, 0]
    table_sent = sent_bases[0, 0]
    sample_list = sample_ids[0]
    exps_all = exponents[0]
    last_grads = cotangent[0]
    down_proj = w_down[0]
    up_proj = w_up[0]
    scale_gain = norm_gain[0]
    tick_count = micro_count + sections - 1
    tick_list = jnp.arange(tick_count, dtype=jnp.int32)

    def forward_tick(loop_state, tick_number):
        arrived, rebuilt_store, hidden_store, inner_store, active_store = loop_state
        micro_slot = tick_number - my_section
        live_tick = jnp.logical_and(micro_slot >= 0, micro_slot < micro_count)
        position_now = jnp.clip(micro_slot, 0, micro_count - 1)
        sample_row = pick(sample_list, position_now)
        block_exps = pick(exps_all, position_now)
        received = pick(table_in, sample_row)
        sent_copy = pick(table_sent, sample_row)
        rebuilt_now = (received.astype(jnp.float32) + dequantize(arrived, block_exps)).astype(
            jnp.bfloat16
        )
        hidden, inner, active, output = layer_forward(rebuilt_now, down_proj, up_proj, scale_gain)
        outgoing = quantize(output - sent_copy.astype(jnp.float32), block_exps)
        rebuilt_store = keep_slot(rebuilt_store, rebuilt_now, position_now, live_tick)
        hidden_store = keep_slot(hidden_store, hidden, position_now, live_tick)
        inner_store = keep_slot(inner_store, inner, position_now, live_tick)
        active_store = keep_slot(active_store, active, position_now, live_tick)
        next_arrived = from_behind(outgoing, "section", 1)
        return ((next_arrived, rebuilt_store, hidden_store, inner_store, active_store), None)

    forward_start = (
        jnp.zeros((row_count, feature_count), jnp.bfloat16),
        jnp.zeros((micro_count, row_count, feature_count), jnp.bfloat16),
        jnp.zeros((micro_count, row_count, feature_count), jnp.bfloat16),
        jnp.zeros((micro_count, row_count, adapter), jnp.float32),
        jnp.zeros((micro_count, row_count, adapter), jnp.bfloat16),
    )
    forward_end, _ = lax.scan(forward_tick, forward_start, tick_list)
    _, rebuilt_store, hidden_store, inner_store, active_store = forward_end

    def backward_tick(loop_state, tick_number):
        arriving, gain_total, grad_inner_store, grad_out_store = loop_state
        micro_slot = tick_number - (sections - 1 - my_section)
        live_tick = jnp.logical_and(micro_slot >= 0, micro_slot < micro_count)
        position_now = jnp.clip(micro_slot, 0, micro_count - 1)
        grad_out = jnp.where(my_section == sections - 1, pick(last_grads, position_now), arriving)
        normed, spread = normalize(pick(rebuilt_store, position_now))
        inner = pick(inner_store, position_now)
        grad_input, grad_inner, gain_terms = layer_backward(
            grad_out, normed, spread, inner, down_proj, up_proj, scale_gain
        )
        gain_total = gain_total + jnp.where(live_tick, gain_terms, 0.0)
        grad_inner_store = keep_slot(grad_inner_store, grad_inner, position_now, live_tick)
        grad_out_store = keep_slot(grad_out_store, grad_out, position_now, live_tick)
        returned = from_behind(grad_input, "section", -1)
        return ((returned, gain_total, grad_inner_store, grad_out_store), None)

    backward_start = (
        jnp.zeros((row_count, feature_count), jnp.bfloat16),
        jnp.zeros((feature_count,), jnp.float32),
        jnp.zeros((micro_count, row_count, adapter), jnp.bfloat16),
        jnp.zeros((micro_count, row_count, feature_count), jnp.bfloat16),
    )
    backward_end, _ = lax.scan(backward_tick, backward_start, tick_list)
    _, gain_total, grad_inner_store, grad_out_store = backward_end
    tokens = micro_count * row_count
    hidden_flat = hidden_store.reshape(tokens, feature_count)
    active_flat = active_store.reshape(tokens, adapter)
    grad_inner_flat = grad_inner_store.reshape(tokens, adapter)
    grad_out_flat = grad_out_store.reshape(tokens, feature_count)
    local_down = contract_rows(hidden_flat, grad_inner_flat)
    local_up = contract_rows(active_flat, grad_out_flat)
    grad_down, grad_up, gain_grad = (
        lax.psum_scatter(
            local_down.astype(jnp.bfloat16), "dp", scatter_dimension=0, tiled=True
        ).astype(jnp.float32),
        lax.psum_scatter(
            local_up.astype(jnp.bfloat16), "dp", scatter_dimension=1, tiled=True
        ).astype(jnp.float32),
        lax.psum_scatter(
            gain_total.astype(jnp.bfloat16), "dp", scatter_dimension=0, tiled=True
        ).astype(jnp.float32),
    )
    return (rebuilt_store[None, None], grad_down[None], grad_up[None], gain_grad[None])


def solution(mesh):
    return jax.shard_map(
        on_device,
        mesh=mesh,
        in_specs=(
            P("section", "dp", None, None, None),
            P("section", "dp", None, None, None),
            P("dp", None),
            P("dp", None, None, None),
            P("dp", None, None, None),
            P("section", None, None),
            P("section", None, None),
            P("section", None),
        ),
        out_specs=(
            P("section", "dp", None, None, None),
            P("section", "dp", None),
            P("section", None, "dp"),
            P("section", "dp"),
        ),
        check_vma=False,
    )
```

profile of v0, /device:TPU:0, one launch (start us, length us, event | category | flops | bytes accessed | tf_op | source)
XLA Modules:
  0.0 1427.8 jit_solution(2485778930692705312)
XLA Ops:
  12.3 615.9 %while.37 = (s32[]{:T(128)}, bf16[24,8192]{1,0:T(8,128)(2,1)}, bf16[8,24,8192]{2,1,0:T(8,128)(2,1)S(1)}, bf16[8,24,8192]{2,1,0:T(8,128)(2,1)}, f32[8,24,256]{2,1...) while((s32[]{:T(128)}, bf16[24,8192]{1,0:T(8,128)(2,1)}, ...), condition=%wide.region_2.3_spmd, body=%wide.region_0.2_spmd.sunk | while | flops 206321696 | bytes 38689736 | solution.py:129
  632.1 568.0 %while.38 = (s32[]{:T(128)}, bf16[24,8192]{1,0:T(8,128)(2,1)}, f32[8192]{0:T(1024)}, bf16[8,24,256]{2,1,0:T(8,128)(2,1)}, bf16[8,24,8192]{2,1,0:T(8,128)(2,1)}, ...) while((s32[]{:T(128)}, bf16[24,8192]{1,0:T(8,128)(2,1)}, ...), condition=%wide.region_7.8_spmd.clone, body=%wide.region_3.7_spmd.clone.sunk | while | flops 205533216 | bytes 35423984 | solution.py:155
  670.0 9.4 collective-permute-done.1
  718.6 8.8 collective-permute-done.1
  766.7 8.8 collective-permute-done.1
  814.8 8.8 collective-permute-done.1
  839.9 8.7 collective-permute-done.1
  864.9 8.7 collective-permute-done.1
  890.0 8.7 collective-permute-done.1
  915.0 8.7 collective-permute-done.1
  940.0 8.7 collective-permute-done.1
  965.1 8.7 collective-permute-done.1
  990.1 8.7 collective-permute-done.1
  1015.2 8.8 collective-permute-done.1
  1040.4 8.7 collective-permute-done.1
  1065.4 8.9 collective-permute-done.1
  1090.6 8.5 collective-permute-done.1
  1115.5 8.9 collective-permute-done.1
  1140.7 8.6 collective-permute-done.1
  1165.6 8.7 collective-permute-done.1
  1190.6 8.7 collective-permute-done.1
  1214.5 41.9 %all-reduce = bf16[8192]{0:T(1024)(128)(2,1)S(1)} all-reduce(bf16[8192]{0:T(1024)(128)(2,1)S(1)} %convert_element_type.80), channel_id=4, replica_groups=mesh['section'=16,'dp'=8] {'dp'}, use_global_device_ids=true, to_apply=%region_10.11.clone | all-reduce | flops 8192 | bytes 32768
  1257.0 74.2 %reduce-scatter.5.cloned.1.call-done = bf16[256,1024]{1,0:T(8,128)(2,1)} async-done(((bf16[256,8192]{1,0:T(8,128)(2,1)}), bf16[256,1024]{1,0:T(8,128)(2,1)}) %reduce-scatter.5.cloned.1.call-update) | async-done | bytes 524304 | tf_op jit(solution)/shard_map/reduce_scatter | solution.py:168
  1333.3 85.5 %reduce-scatter.3.cloned.1.call-done = bf16[1024,256]{1,0:T(8,128)(2,1)} async-done(((bf16[8192,256]{1,0:T(8,128)(2,1)}), bf16[1024,256]{1,0:T(8,128)(2,1)}) %reduce-scatter.3.cloned.1.call-update) | async-done | bytes 524304 | tf_op jit(solution)/shard_map/reduce_scatter | solution.py:165
  (1048 shorter events, 969.0 us)
Async XLA Ops:
  7.2 1324.0 %reduce-scatter.5.cloned.1.call-start = ((), (), s32[]{:S(2)}) async-start(), calls=%async_computation.3 | async-start | bytes 4718592 | tf_op jit(solution)/shard_map/reduce_scatter | solution.py:168
  418.4 11.4 collective-permute-start
  446.6 11.4 collective-permute-start
  474.9 11.4 collective-permute-start
  531.3 11.4 collective-permute-start
  559.6 11.4 collective-permute-start
  587.8 11.4 collective-permute-start
  616.0 11.4 collective-permute-start
  667.4 12.0 collective-permute-start.1
  716.0 11.5 collective-permute-start.1
  764.0 11.5 collective-permute-start.1
  812.1 11.5 collective-permute-start.1
  837.2 11.4 collective-permute-start.1
  862.3 11.4 collective-permute-start.1
  887.3 11.4 collective-permute-start.1
  912.3 11.4 collective-permute-start.1
  937.4 11.4 collective-permute-start.1
  962.4 11.4 collective-permute-start.1
  987.5 11.4 collective-permute-start.1
  1012.5 11.5 collective-permute-start.1
  1062.7 11.6 collective-permute-start.1
  1112.8 11.6 collective-permute-start.1
  1188.0 11.4 collective-permute-start.1
  1206.4 212.4 %reduce-scatter.3.cloned.1.call-start = ((), (), s32[]{:S(2)}) async-start(), calls=%async_computation.2 | async-start | bytes 4718592 | tf_op jit(solution)/shard_map/reduce_scatter | solution.py:165
  (190 other events, 806.6 us)
Sparse Core Ops, SparseCore 0:
  1206.6 124.5 reduce-scatter.4
  1335.5 83.2 reduce-scatter.2
where the time goes:
time: 1440 us; the launch traced here: 1430 us
  waiting for transfers between devices  353 us (25%)
  matrix products  292 us (20%)
  other arithmetic  243 us (17%)
  local copies, waits for them, and re-layouts  243 us (17%)
  starting transfers between devices  164 us (11%)
  loops' own time  75.5 us (5%)
  blocking collectives  41.9 us (3%)
  between operations  14.7 us (1%)
    ppermute x46, waiting for transfers between devices, from_behind(): lax.ppermute(value, axis, [(source, source + steps) for source in range(i...  194 us
    ppermute x46, starting transfers between devices, from_behind(): lax.ppermute(value, axis, [(source, source + steps) for source in range(i...  164 us
    dynamic_update_slice x92, other arithmetic, keep_slot(): return lax.dynamic_update_index_in_dim(buffer, chosen, position_now, 0)  143 us
    dynamic_slice x161, local copies, waits for them, and re-layouts, pick(): lax.dynamic_index_in_dim(stored_table, position_now, 0, keepdims=False)  113 us
    dot_general x23, matrix products, layer_backward(): lax.dot_general(grad_out, up_proj, (((1,), (1,)), ((), ())), preferred_el...  91.8 us
    reduce_scatter x1, waiting for transfers between devices, on_device(): lax.psum_scatter(local_down.astype(jnp.bfloat16), 'dp', scatter_dimension...  85.5 us
    dot_general x23, matrix products, layer_forward(): inner = jnp.dot(hidden, down_proj, preferred_element_type=jnp.float32)  84.9 us
    reduce_scatter x1, waiting for transfers between devices, on_device(): lax.psum_scatter(local_up.astype(jnp.bfloat16), 'dp', scatter_dimension=1...  74.2 us
  transfers between devices with their start and end apart: 48, of which 25 were waited for; matrix products, arithmetic and copies ran while one was open for 9% of the time, Pallas kernels for 0%

commit v1 on v0

v1 whole, which is shorter than its diff:
```python
import functools

import jax
import jax.numpy as jnp
from jax import lax
from jax.experimental import pallas as pl
from jax.experimental.pallas import tpu as pltpu
from jax.sharding import PartitionSpec as P

BLOCK = 128
LIMIT = 448.0
EPSILON = 1e-05
RC = 16
PIECES = 8
MESH = pl.DeviceIdType.MESH
F32 = jnp.float32
BF16 = jnp.bfloat16


def gather_kernel(ids, in_ref, sent_ref, exps_ref, base_ref, copy_ref, lim_ref):
    del ids
    base_ref[...] = in_ref[...]
    copy_ref[...] = sent_ref[...]
    blocks, features = exps_ref.shape[-1], lim_ref.shape[-1]
    bound = (LIMIT * jnp.exp2(exps_ref[0].astype(F32)).astype(BF16).astype(F32)).astype(BF16)
    owner = lax.broadcasted_iota(jnp.int32, (blocks, features), 1) // BLOCK
    row = lax.broadcasted_iota(jnp.int32, (blocks, features), 0)
    spread = jnp.where(owner == row, 1.0, 0.0).astype(BF16)
    lim_ref[0] = jnp.dot(bound, spread, preferred_element_type=F32).astype(BF16)


def gather(ids, in_table, sent_table, exps):
    micro, rows, blocks = exps.shape
    features = in_table.shape[-1]
    picked = pl.BlockSpec((1, rows, features), lambda m, ids: (ids[m], 0, 0))
    placed = pl.BlockSpec((1, rows, features), lambda m, ids: (m, 0, 0))
    shape = jax.ShapeDtypeStruct((micro, rows, features), BF16)
    return pl.pallas_call(
        gather_kernel,
        out_shape=(shape,) * 3,
        grid_spec=pltpu.PrefetchScalarGridSpec(
            num_scalar_prefetch=1,
            grid=(micro,),
            in_specs=[picked, picked, pl.BlockSpec((1, rows, blocks), lambda m, ids: (m, 0, 0))],
            out_specs=(placed,) * 3,
        ),
        compiler_params=pltpu.CompilerParams(vmem_limit_bytes=32 * 2**20),
        name="gather_bases",
    )(ids, in_table, sent_table, exps)


def relay_kernel(
    sections, replicas,
    base_hbm, sent_hbm, lim_hbm, cot_hbm, wd_hbm, wu_hbm, gain,
    reb_hbm, pdown, pup,
    base, delta, sent, lim, go, wd, wu, rb_all, go_all, act_all, gi_all, inner_buf, inv_buf,
    load_sem, f_recv, b_recv, relay_send, x_send, x_recv, out_sem,
):
    s, b = lax.axis_index("section"), lax.axis_index("dp")
    tokens, features = base.shape
    adapter = wd.shape[1]
    chunks = tokens // RC
    width = features // PIECES
    part = features // replicas
    first, last = s == 0, s == sections - 1
    above, below = {"section": s + 1}, {"section": s - 1}

    loads = [
        pltpu.make_async_copy(source, target, load_sem.at[i])
        for i, (source, target) in enumerate(
            [(base_hbm, base), (wd_hbm, wd), (wu_hbm, wu), (sent_hbm, sent), (lim_hbm, lim)]
        )
    ]
    for load in loads:
        load.start()
    cot_load = pltpu.make_async_copy(cot_hbm, go, load_sem.at[5])

    @pl.when(last)
    def _():
        cot_load.start()

    barrier = pltpu.get_barrier_semaphore()

    def greet(device):
        pl.semaphore_signal(barrier, inc=1, device_id=device, device_id_type=MESH)

    @pl.when(jnp.logical_not(first))
    def _():
        greet(below)

    @pl.when(jnp.logical_not(last))
    def _():
        greet(above)

    def peer_of(i):
        return lax.rem(b + 1 + i, replicas)

    def greet_peer(i, _):
        greet({"dp": peer_of(i)})
        return 0

    lax.fori_loop(0, replicas - 1, greet_peer, 0)

    @pl.when(first)
    def _():
        delta[...] = jnp.zeros_like(delta)

    loads[0].wait()
    loads[1].wait()
    pl.semaphore_wait(
        barrier, replicas - 1 + jnp.where(first, 0, 1) + jnp.where(last, 0, 1)
    )

    def exchange(kind, source, target, sem_owner, peer):
        return pltpu.make_async_remote_copy(
            src_ref=source, dst_ref=target,
            send_sem=x_send.at[kind, peer], recv_sem=x_recv.at[kind, sem_owner],
            device_id={"dp": peer}, device_id_type=MESH,
        )

    def relay(forward, chunk, piece):
        rows = pl.ds(pl.multiple_of(chunk * RC, RC), RC)
        cols = pl.ds(pl.multiple_of(piece * width, width), width)
        source, target, recv, way, device = (
            (sent, delta, f_recv, 0, above) if forward else (lim, go, b_recv, 1, below)
        )
        return pltpu.make_async_remote_copy(
            src_ref=source.at[rows, cols], dst_ref=target.at[rows, cols],
            send_sem=relay_send.at[way], recv_sem=recv.at[chunk, piece],
            device_id=device, device_id_type=MESH,
        )

    def forward(chunk):
        rows = pl.ds(pl.multiple_of(chunk * RC, RC), RC)

        def take(k, carry):
            acc, squares = carry
            cols = pl.ds(pl.multiple_of(k * width, width), width)

            @pl.when(jnp.logical_not(first))
            def _():
                relay(True, chunk, k).wait_recv()

            rebuilt = (base[rows, cols].astype(F32) + delta[rows, cols].astype(F32)).astype(BF16)
            base[rows, cols] = rebuilt
            wide = rebuilt.astype(F32)
            square = wide * wide
            for i in range(width // BLOCK):
                squares = squares + square[:, i * BLOCK:(i + 1) * BLOCK]
            hidden = (wide * gain[:, cols]).astype(BF16)
            return acc + jnp.dot(hidden, wd[cols, :], preferred_element_type=F32), squares

        acc, squares = lax.fori_loop(
            0, PIECES, take, (jnp.zeros((RC, adapter), F32), jnp.zeros((RC, BLOCK), F32))
        )
        spread = jnp.sqrt(jnp.sum(squares, axis=1, keepdims=True) / features + EPSILON)
        inverse = 1.0 / spread
        inner = acc * inverse
        active = (inner / (1.0 + jnp.exp(-inner))).astype(BF16)
        inner_buf[rows, :] = inner
        inv_buf[rows, :] = jnp.broadcast_to(inverse, (RC, BLOCK))
        act_all[b, rows, :] = active

        @pl.when(chunk == 0)
        def _():
            for load in loads[2:]:
                load.wait()

        @pl.when(jnp.logical_not(last))
        def _():
            def give(k, _):
                cols = pl.ds(pl.multiple_of(k * width, width), width)
                output = base[rows, cols].astype(F32) + jnp.dot(
                    active, wu[:, cols], preferred_element_type=F32
                )
                bound = lim[rows, cols].astype(F32)
                difference = output - sent[rows, cols].astype(F32)
                sent[rows, cols] = jnp.clip(difference, -bound, bound).astype(BF16)
                relay(True, chunk, k).start()
                return 0

            lax.fori_loop(0, PIECES, give, 0)

        pltpu.make_async_copy(base.at[rows, :], reb_hbm.at[rows, :], out_sem).start()
        rb_all[b, rows, :] = base[rows, pl.ds(pl.multiple_of(b * part, part), part)]

        def share(i, _):
            peer = peer_of(i)
            cols = pl.ds(pl.multiple_of(peer * part, part), part)
            exchange(0, base.at[rows, cols], rb_all.at[b, rows], b, peer).start()
            exchange(1, act_all.at[b, rows], act_all.at[b, rows], b, peer).start()
            return 0

        lax.fori_loop(0, replicas - 1, share, 0)

    def backward(chunk):
        rows = pl.ds(pl.multiple_of(chunk * RC, RC), RC)

        @pl.when(jnp.logical_and(last, chunk == 0))
        def _():
            cot_load.wait()

        def take(k, acc):
            cols = pl.ds(pl.multiple_of(k * width, width), width)

            @pl.when(jnp.logical_not(last))
            def _():
                relay(False, chunk, k).wait_recv()

            return acc + lax.dot_general(
                go[rows, cols], wu[:, cols], (((1,), (1,)), ((), ())), preferred_element_type=F32
            )

        grad_active = lax.fori_loop(0, PIECES, take, jnp.zeros((RC, adapter), F32))
        inner, inverse = inner_buf[rows, :], inv_buf[rows, :][:, :1]
        sigma = 1.0 / (1.0 + jnp.exp(-inner))
        grad_inner = grad_active * sigma * (1.0 + inner * (1.0 - sigma))
        scaled = (grad_inner * inverse).astype(BF16)
        gi_all[b, rows, :] = scaled
        drift = jnp.sum(grad_inner * inner, axis=1, keepdims=True) / features * inverse * inverse

        @pl.when(jnp.logical_not(first))
        def _():
            def give(k, _):
                cols = pl.ds(pl.multiple_of(k * width, width), width)
                grad = lax.dot_general(
                    scaled, wd[cols, :], (((1,), (1,)), ((), ())), preferred_element_type=F32
                )
                lim[rows, cols] = (
                    go[rows, cols].astype(F32)
                    + grad * gain[:, cols]
                    - base[rows, cols].astype(F32) * drift
                ).astype(BF16)
                relay(False, chunk, k).start()
                return 0

            lax.fori_loop(0, PIECES, give, 0)

        go_all[b, rows, :] = go[rows, pl.ds(pl.multiple_of(b * part, part), part)]

        def share(i, _):
            peer = peer_of(i)
            cols = pl.ds(pl.multiple_of(peer * part, part), part)
            exchange(2, go.at[rows, cols], go_all.at[b, rows], b, peer).start()
            exchange(3, gi_all.at[b, rows], gi_all.at[b, rows], b, peer).start()
            return 0

        lax.fori_loop(0, replicas - 1, share, 0)

    def tick(t, _):
        f_chunk = t - s
        b_chunk = t - (2 * sections - 2 - s)

        @pl.when(jnp.logical_and(f_chunk >= 0, f_chunk < chunks))
        def _():
            forward(f_chunk)

        @pl.when(jnp.logical_and(b_chunk >= 0, b_chunk < chunks))
        def _():
            backward(b_chunk)

        return 0

    lax.fori_loop(0, 2 * sections - 2 + chunks, tick, 0)

    def contract(p):
        dims = (((0,), (0,)), ((), ()))
        return (
            lax.dot_general(gi_all[p], rb_all[p], dims, preferred_element_type=F32),
            lax.dot_general(act_all[p], go_all[p], dims, preferred_element_type=F32),
        )

    pdown[...], pup[...] = contract(b)

    def collect(i, _):
        peer = lax.rem(b + replicas - 1 - i, replicas)
        for kind, ref in enumerate((rb_all, act_all, go_all, gi_all)):
            exchange(kind, ref.at[peer], ref.at[peer], peer, peer).wait_recv()
        down, up = contract(peer)
        pdown[...] += down
        pup[...] += up
        return 0

    lax.fori_loop(0, replicas - 1, collect, 0)

    def settle(i, _):
        peer = peer_of(i)
        for kind, ref in enumerate((rb_all, act_all, go_all, gi_all)):
            exchange(kind, ref.at[peer], ref.at[peer], peer, peer).wait_send()
        return 0

    lax.fori_loop(0, replicas - 1, settle, 0)

    def sent_all(buffer, way, device):
        pltpu.make_async_remote_copy(
            src_ref=buffer, dst_ref=buffer, send_sem=relay_send.at[way], recv_sem=f_recv.at[0, 0],
            device_id=device, device_id_type=MESH,
        ).wait_send()

    @pl.when(jnp.logical_not(last))
    def _():
        sent_all(sent, 0, above)

    @pl.when(jnp.logical_not(first))
    def _():
        sent_all(lim, 1, below)

    pltpu.make_async_copy(base, reb_hbm, out_sem).wait()


def relay_call(sections, replicas, base, sent, lim, cotangent, w_down, w_up, gain):
    tokens, features = base.shape
    adapter = w_down.shape[1]
    part = features // replicas
    chunks = tokens // RC
    whole = pltpu.VMEM((tokens, features), BF16)
    anywhere = pl.BlockSpec(memory_space=pl.ANY)
    in_vmem = pl.BlockSpec(memory_space=pltpu.VMEM)
    dma = pltpu.SemaphoreType.DMA
    flops = 12 * tokens * features * adapter
    return pl.pallas_call(
        functools.partial(relay_kernel, sections, replicas),
        out_shape=(
            jax.ShapeDtypeStruct((tokens, features), BF16),
            jax.ShapeDtypeStruct((adapter, part), F32),
            jax.ShapeDtypeStruct((adapter, part), F32),
        ),
        in_specs=[anywhere] * 6 + [in_vmem],
        out_specs=(anywhere, in_vmem, in_vmem),
        scratch_shapes=[
            whole, whole, whole, whole, whole,
            pltpu.VMEM((features, adapter), BF16),
            pltpu.VMEM((adapter, features), BF16),
            pltpu.VMEM((replicas, tokens, part), BF16),
            pltpu.VMEM((replicas, tokens, part), BF16),
            pltpu.VMEM((replicas, tokens, adapter), BF16),
            pltpu.VMEM((replicas, tokens, adapter), BF16),
            pltpu.VMEM((tokens, adapter), F32),
            pltpu.VMEM((tokens, BLOCK), F32),
            dma((6,)), dma((chunks, PIECES)), dma((chunks, PIECES)), dma((2,)),
            dma((4, replicas)), dma((4, replicas)), dma,
        ],
        compiler_params=pltpu.CompilerParams(
            collective_id=0, has_side_effects=True, vmem_limit_bytes=56 * 2**20
        ),
        cost_estimate=pl.CostEstimate(
            flops=flops, bytes_accessed=24 * 2**20, transcendentals=0
        ),
        name="relay",
    )(base, sent, lim, cotangent, w_down, w_up, gain)


def solution(mesh):
    sections, replicas = mesh.shape["section"], mesh.shape["dp"]

    def on_device(in_bases, sent_bases, sample_ids, exponents, cotangent, w_down, w_up, norm_gain):
        micro, rows, features = cotangent.shape[1:]
        tokens = micro * rows
        part = features // replicas
        base, sent, lim = gather(sample_ids[0], in_bases[0, 0], sent_bases[0, 0], exponents[0])
        flat = (tokens, features)
        rebuilt, pdown, pup = relay_call(
            sections, replicas, base.reshape(flat), sent.reshape(flat), lim.reshape(flat),
            cotangent[0].reshape(flat), w_down[0], w_up[0], norm_gain,
        )
        start = lax.axis_index("dp") * part
        gain = lax.dynamic_slice_in_dim(norm_gain[0], start, part, 0)
        down = lax.dynamic_slice_in_dim(w_down[0], start, part, 0)
        plain = pdown.T
        grad_down = plain * gain[:, None]
        gain_grad = jnp.sum(plain * down.astype(F32), axis=1)
        return (
            rebuilt.reshape(1, 1, micro, rows, features),
            grad_down[None],
            pup[None],
            gain_grad[None],
        )

    return jax.shard_map(
        on_device,
        mesh=mesh,
        in_specs=(
            P("section", "dp", None, None, None),
            P("section", "dp", None, None, None),
            P("dp", None),
            P("dp", None, None, None),
            P("dp", None, None, None),
            P("section", None, None),
            P("section", None, None),
            P("section", None),
        ),
        out_specs=(
            P("section", "dp", None, None, None),
            P("section", "dp", None),
            P("section", None, "dp"),
            P("section", "dp"),
        ),
        check_vma=False,
    )
```

time: 1440 us -> 279 us (0.19)
  waiting for transfers between devices: 353 us -> 0 us
  matrix products: 292 us -> 0 us
  Pallas kernels: 0 us -> 257 us
  other arithmetic: 243 us -> 1.99 us
  local copies, waits for them, and re-layouts: 243 us -> 19 us
  starting transfers between devices: 164 us -> 0 us
  loops' own time: 75.5 us -> 0 us
  blocking collectives: 41.9 us -> 0 us
    dot_general x94 -> x0, matrix products: 292 us -> none  [the longest x23 91.8 us: layer_backward(): lax.dot_general(grad_out, up_proj, (((1,), (1,)), ((), ())), preferred_el...]
    pallas_call x0 -> x2, Pallas kernels: none -> 257 us  [the longest x1 254 us: relay_call(): pl.pallas_call(functools.partial(relay_kernel, sections, replicas), out_s...]
    ppermute x46 -> x0, waiting for transfers between devices: 194 us -> none  [from_behind(): lax.ppermute(value, axis, [(source, source + steps) for source in range(i...]
    dynamic_slice x207 -> x2, local copies, waits for them, and re-layouts: 168 us -> 1.78 us  [the longest x1 1.08 us: on_device(): down = lax.dynamic_slice_in_dim(w_down[0], start, part, 0)]
    ppermute x46 -> x0, starting transfers between devices: 164 us -> none  [from_behind(): lax.ppermute(value, axis, [(source, source + steps) for source in range(i...]
    reduce_scatter x2 -> x0, waiting for transfers between devices: 160 us -> none  [the longest x1 85.5 us: on_device(): lax.psum_scatter(local_down.astype(jnp.bfloat16), 'dp', scatter_dimension...]
    dynamic_update_slice x92 -> x0, other arithmetic: 143 us -> none  [keep_slot(): return lax.dynamic_update_index_in_dim(buffer, chosen, position_now, 0)]
    another operation x2 -> x0, loops' own time: 75.5 us -> none  [the longest x1 59.4 us: on_device(): forward_end, _ = lax.scan(forward_tick, forward_start, tick_list)]
  transfers between devices with their start and end apart: 48 -> 0, of which waited for: 25 -> 0; matrix products, arithmetic and copies ran while one was open for 9% -> 0% of each run, Pallas kernels for 0% -> 0%
where the time goes in v1:
time: 279 us; the launch traced here: 278 us
  Pallas kernels  257 us (92%)
  local copies, waits for them, and re-layouts  19 us (7%)
    pallas_call x1, Pallas kernels, relay_call(): pl.pallas_call(functools.partial(relay_kernel, sections, replicas), out_s...  254 us
    unnamed x20, local copies, waits for them, and re-layouts  17.2 us

profile of v1, /device:TPU:0, one launch (start us, length us, event | category | flops | bytes accessed | tf_op | source)
XLA Modules:
  0.0 278.5 jit_solution(8128175243884167771)
XLA Ops:
  0.6 0.0 copy-start
  0.6 2.1 copy-done
  2.7 0.0 copy-start.1
  2.7 2.1 copy-done.1
  4.9 0.0 copy-start.5
  4.9 0.9 copy-done.5
  5.8 0.0 copy-start.6
  5.8 0.7 copy-done.6
  6.4 3.2 %gather_bases.1 = (bf16[8,24,8192]{2,1,0:T(8,128)(2,1)S(1)}, bf16[8,24,8192]{2,1,0:T(8,128)(2,1)S(1)}, bf16[8,24,8192]{2,1,0:T(8,128)(2,1)S(1)}) custom-call(s32[8]{0:T(128)S(1)} %bitcast.30, bf16[10,24,8192]{2,1,0:T(8,128)(2,1)S(1)} %bitcast.24, bf16[10,24,8192]{2,1,0:T(8,128)(2,1)S(1)} %bitcast.25, s32[8,24,64]{2,1,0:T(8,128)S(1)} %bitcast.29), custom_call_target="tpu_custom_call" | custom-call | tf_op jit(solution)/shard_map/gather_bases/pallas_call | solution.py:38
  9.7 0.0 copy-start.2
  9.7 1.7 copy-done.2
  11.3 0.0 copy-start.3
  11.3 1.6 copy-done.3
  13.0 0.0 copy-start.4
  13.0 1.7 copy-done.4
  14.7 253.6 %relay.1 = (bf16[192,8192]{1,0:T(8,128)(2,1)}, f32[256,1024]{1,0:T(8,128)}, f32[256,1024]{1,0:T(8,128)}) custom-call(bf16[192,8192]{1,0:T(8,128)(2,1)} %bitcast.26, bf16[192,8192]{1,0:T(8,128)(2,1)} %bitcast.27, bf16[192,8192]{1,0:T(8,128)(2,1)} %bitcast.28, bf16[192,8192]{1,0:T(8,128)(2,1)} %bitcast.33, bf16[8192,256]{1,0:T(8,128)(2,1)} %bitcast.31, ...), custom_call_target="tpu_custom_call" | custom-call | flops 4831838208 | bytes 25165824 | tf_op jit(solution)/shard_map/relay/pallas_call | solution.py:321
  268.3 1.1 constant_dynamic-slice_fusion
  269.3 0.2 copy.14
  269.6 0.7 constant_dynamic-slice_fusion.1
  270.2 2.0 fusion
  272.2 1.3 copy.13
  273.5 3.9 %copy.17 = bf16[1,1,8,24,8192]{4,3,2,1,0:T(8,128)(2,1)} copy(bf16[1,1,8,24,8192]{4,3,2,1,0:T(8,128)(2,1)} %bitcast.34) | data formatting | bytes 6291456
  277.5 0.0 copy-done.7
  277.5 1.0 copy.18
  (1 shorter events, 0.0 us)
Async XLA Ops:
  0.6 2.1 copy-start
  2.7 2.1 copy-start.1
  4.9 0.9 copy-start.5
  5.8 0.7 copy-start.6
  9.7 1.7 copy-start.2
  11.3 1.6 copy-start.3
  13.0 1.7 copy-start.4
  273.5 3.9 %copy-start.7 = (f32[256,1024]{1,0:T(8,128)S(1)}, f32[256,1024]{1,0:T(8,128)}, u32[]{:S(2)}) copy-start(f32[256,1024]{1,0:T(8,128)} %get-tuple-element.15) | copy-start | bytes 3145732

commit v2 on v1

v2 whole, which is shorter than its diff:
```python
import functools

import jax
import jax.numpy as jnp
from jax import lax
from jax.experimental import pallas as pl
from jax.experimental.pallas import tpu as pltpu
from jax.sharding import PartitionSpec as P

BLOCK = 128
LIMIT = 448.0
EPSILON = 1e-05
RC = 16
PIECES = 2
UNIT = 2
GROUPS = 3
MESH = pl.DeviceIdType.MESH
F32 = jnp.float32
BF16 = jnp.bfloat16


def relay_kernel(
    sections, replicas, slab,
    ids, exps_hbm, in_hbm, sent_hbm, cot_hbm, wd_hbm, wu_hbm, gain_hbm,
    reb_hbm, pdown, pup, pgain,
    in_table, sent_table, exps, gain, base, sent, delta, lim, go, zeros, wd, wu, wd_t, wu_t,
    rb_all, go_all, act_all, gi_all, inner_buf, inv_buf,
    load_sem, f_recv, b_recv, relay_send, x_send, x_recv, out_sem,
):
    s, b = lax.axis_index("section"), lax.axis_index("dp")
    tokens, features = base.shape
    adapter = wd.shape[1]
    chunks = tokens // RC
    width = features // PIECES
    part = features // replicas
    per_group = chunks // GROUPS
    first, last = s == 0, s == sections - 1
    above, below = {"section": s + 1}, {"section": s - 1}

    pairs = (
        (exps_hbm, exps), (gain_hbm, gain), (in_hbm, in_table), (wd_hbm, wd),
        (wu_hbm, wu), (sent_hbm, sent_table),
    )
    loads = [
        pltpu.make_async_copy(source, target, load_sem.at[i])
        for i, (source, target) in enumerate(pairs)
    ]
    for load in loads:
        load.start()

    def rows_of(chunk):
        return pl.ds(pl.multiple_of(chunk * RC, RC), RC)

    def cols_of(piece):
        return pl.ds(pl.multiple_of(piece * width, width), width)

    zeros[...] = jnp.zeros_like(zeros)

    @pl.when(first)
    def _():
        def fill(chunk, _):
            for k in range(PIECES):
                pltpu.make_async_copy(
                    zeros, delta.at[rows_of(chunk), cols_of(k)], f_recv.at[chunk, k]
                ).start()
            return 0

        lax.fori_loop(0, chunks, fill, 0)

    @pl.when(last)
    def _():
        def fill(chunk, _):
            for k in range(PIECES):
                block = (rows_of(chunk), cols_of(k))
                pltpu.make_async_copy(
                    cot_hbm.at[block], go.at[block], b_recv.at[chunk, k]
                ).start()
            return 0

        lax.fori_loop(0, chunks, fill, 0)

    barrier = pltpu.get_barrier_semaphore()

    def greet(device):
        pl.semaphore_signal(barrier, inc=1, device_id=device, device_id_type=MESH)

    @pl.when(jnp.logical_not(first))
    def _():
        greet(below)

    @pl.when(jnp.logical_not(last))
    def _():
        greet(above)

    def peer_of(i):
        return lax.rem(b + 1 + i, replicas)

    def greet_peer(i, _):
        greet({"dp": peer_of(i)})
        return 0

    lax.fori_loop(0, replicas - 1, greet_peer, 0)

    loads[0].wait()
    blocks = features // BLOCK
    bound = (LIMIT * jnp.exp2(exps[...].astype(F32)).astype(BF16).astype(F32)).astype(BF16)
    for k in range(PIECES):
        owner = lax.broadcasted_iota(jnp.int32, (blocks, width), 1) // BLOCK + k * (width // BLOCK)
        row = lax.broadcasted_iota(jnp.int32, (blocks, width), 0)
        spread = jnp.where(owner == row, 1.0, 0.0).astype(BF16)
        lim[:, cols_of(k)] = jnp.dot(bound, spread, preferred_element_type=F32).astype(BF16)

    def transpose_weights():
        step = features // 8
        for i in range(8):
            span = pl.ds(i * step, step)
            wd_t[:, span] = wd[span, :].T
            wu_t[span, :] = wu[:, span].T

    shape = (tokens, in_table.shape[0])
    row, column = (lax.broadcasted_iota(jnp.int32, shape, axis) for axis in (0, 1))
    wanted = jnp.zeros(shape, jnp.int32)
    for m in range(tokens // slab):
        inside = jnp.logical_and(row >= m * slab, row < (m + 1) * slab)
        wanted = jnp.where(inside, row + (ids[0, m] - m) * slab, wanted)
    picks = jnp.where(column == wanted, 1.0, 0.0).astype(BF16)

    def pick(table, target):
        step = features // 8

        def some(i, _):
            cols = pl.ds(pl.multiple_of(i * step, step), step)
            target[:, cols] = jnp.dot(
                picks, table[:, cols], preferred_element_type=F32
            ).astype(BF16)
            return 0

        lax.fori_loop(0, 8, some, 0)

    loads[1].wait()
    loads[2].wait()
    pick(in_table, base)

    @pl.when(jnp.logical_not(first))
    def _():
        loads[5].wait()
        pick(sent_table, sent)

    loads[3].wait()
    pl.semaphore_wait(
        barrier, replicas - 1 + jnp.where(first, 0, 1) + jnp.where(last, 0, 1)
    )

    def exchange(kind, source, target, group, owner, peer):
        return pltpu.make_async_remote_copy(
            src_ref=source, dst_ref=target,
            send_sem=x_send.at[kind, peer], recv_sem=x_recv.at[kind, group, owner],
            device_id={"dp": peer}, device_id_type=MESH,
        )

    def relay(forward, chunk, piece):
        block = (rows_of(chunk), cols_of(piece))
        source, target, recv, way, device = (
            (delta, delta, f_recv, 0, above) if forward else (lim, go, b_recv, 1, below)
        )
        return pltpu.make_async_remote_copy(
            src_ref=source.at[block], dst_ref=target.at[block],
            send_sem=relay_send.at[way], recv_sem=recv.at[chunk, piece],
            device_id=device, device_id_type=MESH,
        )

    def place(chunk, count):
        group = chunk // per_group
        offset = pl.multiple_of((chunk % per_group) * RC, RC)
        return group, pl.ds(offset, count * RC)

    def share(kinds, buffer, start, count):
        rows = pl.ds(pl.multiple_of(start * RC, RC), count * RC)
        group, spot = place(start, count)
        wide, narrow = (rb_all, act_all) if kinds == 0 else (go_all, gi_all)

        def to_peer(i, _):
            peer = peer_of(i)
            cols = pl.ds(pl.multiple_of(peer * part, part), part)
            target = wide.at[group, b, spot]
            exchange(kinds, buffer.at[rows, cols], target, group, b, peer).start()
            source = narrow.at[group, b, spot]
            exchange(kinds + 1, source, source, group, b, peer).start()
            return 0

        lax.fori_loop(0, replicas - 1, to_peer, 0)

    def share_forward():
        def one(group, _):
            share(0, base, group * per_group, per_group)
            return 0

        lax.fori_loop(0, GROUPS, one, 0)

    own = pl.ds(pl.multiple_of(b * part, part), part)
    early = s < sections // 4
    pause_mid, pause_end = s < sections // 2, s >= sections * 3 // 4
    within = jnp.logical_not(jnp.logical_or(pause_mid, pause_end))

    def forward(chunk):
        rows = rows_of(chunk)
        group, spot = place(chunk, 1)

        def take(k, carry):
            acc, squares = carry
            cols = cols_of(k)
            relay(True, chunk, k).wait_recv()
            rebuilt = (base[rows, cols].astype(F32) + delta[rows, cols].astype(F32)).astype(BF16)
            base[rows, cols] = rebuilt
            wide = rebuilt.astype(F32)
            square = wide * wide
            for i in range(width // BLOCK):
                squares = squares + square[:, i * BLOCK:(i + 1) * BLOCK]
            hidden = (wide * gain[:, cols]).astype(BF16)
            return acc + jnp.dot(hidden, wd[cols, :], preferred_element_type=F32), squares

        acc, squares = lax.fori_loop(
            0, PIECES, take, (jnp.zeros((RC, adapter), F32), jnp.zeros((RC, BLOCK), F32))
        )
        spread = jnp.sqrt(jnp.sum(squares, axis=1, keepdims=True) / features + EPSILON)
        inverse = 1.0 / spread
        inner = acc * inverse
        active = (inner / (1.0 + jnp.exp(-inner))).astype(BF16)
        inner_buf[rows, :] = inner
        inv_buf[rows, :] = jnp.broadcast_to(inverse, (RC, BLOCK))
        act_all[group, b, spot, :] = active

        @pl.when(jnp.logical_and(chunk == 0, early))
        def _():
            loads[4].wait()

        @pl.when(jnp.logical_and(chunk == 0, first))
        def _():
            loads[5].wait()
            pick(sent_table, sent)

        @pl.when(jnp.logical_not(last))
        def _():
            def give(k, _):
                cols = cols_of(k)
                output = base[rows, cols].astype(F32) + jnp.dot(
                    active, wu[:, cols], preferred_element_type=F32
                )
                bound = lim[rows, cols].astype(F32)
                difference = output - sent[rows, cols].astype(F32)
                delta[rows, cols] = jnp.clip(difference, -bound, bound).astype(BF16)
                relay(True, chunk, k).start()
                return 0

            lax.fori_loop(0, PIECES, give, 0)

        pltpu.make_async_copy(base.at[rows, :], reb_hbm.at[rows, :], out_sem).start()
        rb_all[group, b, spot, :] = base[rows, own]

        @pl.when(jnp.logical_and(within, chunk % UNIT == UNIT - 1))
        def _():
            share(0, base, chunk - (UNIT - 1), UNIT)

    def backward(chunk):
        rows = rows_of(chunk)
        group, spot = place(chunk, 1)

        def take(k, acc):
            cols = cols_of(k)
            relay(False, chunk, k).wait_recv()
            return acc + jnp.dot(go[rows, cols], wu_t[cols, :], preferred_element_type=F32)

        grad_active = lax.fori_loop(0, PIECES, take, jnp.zeros((RC, adapter), F32))
        inner, inverse = inner_buf[rows, :], inv_buf[rows, :][:, :1]
        sigma = 1.0 / (1.0 + jnp.exp(-inner))
        grad_inner = grad_active * sigma * (1.0 + inner * (1.0 - sigma))
        scaled = (grad_inner * inverse).astype(BF16)
        gi_all[group, b, spot, :] = scaled

        @pl.when(jnp.logical_not(first))
        def _():
            drift = (
                jnp.sum(grad_inner * inner, axis=1, keepdims=True) / features * inverse * inverse
            )

            def give(k, _):
                cols = cols_of(k)
                grad = jnp.dot(scaled, wd_t[:, cols], preferred_element_type=F32)
                lim[rows, cols] = (
                    go[rows, cols].astype(F32)
                    + grad * gain[:, cols]
                    - base[rows, cols].astype(F32) * drift
                ).astype(BF16)
                relay(False, chunk, k).start()
                return 0

            lax.fori_loop(0, PIECES, give, 0)

        go_all[group, b, spot, :] = go[rows, own]

        @pl.when(chunk % UNIT == UNIT - 1)
        def _():
            share(2, go, chunk - (UNIT - 1), UNIT)

    def collect(group):
        def arrive(i, _):
            peer = peer_of(i)
            for kind, ref in enumerate((rb_all, act_all, go_all, gi_all)):
                spot = ref.at[group, peer]
                exchange(kind, spot, spot, group, peer, peer).wait_recv()
            return 0

        lax.fori_loop(0, replicas - 1, arrive, 0)
        dims = (((0,), (0,)), ((), ()))
        rows = replicas * per_group * RC
        wide, narrow = (rows, part), (rows, adapter)
        gi_t = gi_all[group].reshape(narrow)
        act_t = act_all[group].reshape(narrow)
        step = part // 2
        for i in range(2):
            cols = pl.ds(i * step, step)
            pdown[:, cols] += lax.dot_general(
                gi_t, rb_all[group, :, :, cols].reshape(rows, step), dims,
                preferred_element_type=F32,
            )
            pup[:, cols] += lax.dot_general(
                act_t, go_all[group, :, :, cols].reshape(rows, step), dims,
                preferred_element_type=F32,
            )

    pdown[...] = jnp.zeros_like(pdown)
    pup[...] = jnp.zeros_like(pup)
    turn_tick = jnp.where(early, chunks - 1 + s, 0)
    spare = s < sections // 2

    def tick(t, _):
        f_chunk = t - s
        b_chunk = t - (2 * sections - 2 - s)

        @pl.when(jnp.logical_and(t == turn_tick, jnp.logical_not(early)))
        def _():
            loads[4].wait()
            transpose_weights()

        @pl.when(jnp.logical_and(f_chunk >= 0, f_chunk < chunks))
        def _():
            forward(f_chunk)

        @pl.when(jnp.logical_and(pause_mid, f_chunk == chunks - 1))
        def _():
            share_forward()

        @pl.when(jnp.logical_and(t == turn_tick, early))
        def _():
            transpose_weights()

        @pl.when(jnp.logical_and(b_chunk >= 0, b_chunk < chunks))
        def _():
            backward(b_chunk)

        for group in range(GROUPS - 1):
            @pl.when(jnp.logical_and(spare, b_chunk == (group + 2) * per_group - 1))
            def _():
                collect(group)

        return 0

    lax.fori_loop(0, 2 * sections - 2 + chunks, tick, 0)

    @pl.when(pause_end)
    def _():
        share_forward()

    def remaining(group, _):
        collect(group)
        return 0

    lax.fori_loop(jnp.where(spare, GROUPS - 1, 0), GROUPS, remaining, 0)
    summed = pdown[...]
    pdown[...] = summed * gain[:, own]
    pgain[...] = jnp.sum(summed * wd_t[:, own].astype(F32), axis=0, keepdims=True)

    def settle(i, _):
        peer = peer_of(i)
        for kind, ref in enumerate((rb_all, act_all, go_all, gi_all)):
            spot = ref.at[:, peer]
            exchange(kind, spot, spot, 0, peer, peer).wait_send()
        return 0

    lax.fori_loop(0, replicas - 1, settle, 0)

    def sent_all(buffer, way, device):
        pltpu.make_async_remote_copy(
            src_ref=buffer, dst_ref=buffer, send_sem=relay_send.at[way], recv_sem=f_recv.at[0, 0],
            device_id=device, device_id_type=MESH,
        ).wait_send()

    @pl.when(jnp.logical_not(last))
    def _():
        sent_all(delta, 0, above)

    @pl.when(jnp.logical_not(first))
    def _():
        sent_all(lim, 1, below)

    pltpu.make_async_copy(base, reb_hbm, out_sem).wait()


def relay_call(sections, replicas, slab, ids, exps, in_table, sent_table, cotangent, w_down, w_up, gain):
    tokens, features = cotangent.shape
    adapter = w_down.shape[1]
    part = features // replicas
    chunks = tokens // RC
    grouped = (GROUPS, replicas, tokens // GROUPS)
    whole = pltpu.VMEM((tokens, features), BF16)
    anywhere = pl.BlockSpec(memory_space=pl.ANY)
    in_vmem = pl.BlockSpec(memory_space=pltpu.VMEM)
    dma = pltpu.SemaphoreType.DMA
    return pl.pallas_call(
        functools.partial(relay_kernel, sections, replicas, slab),
        out_shape=(
            jax.ShapeDtypeStruct((tokens, features), BF16),
            jax.ShapeDtypeStruct((adapter, part), F32),
            jax.ShapeDtypeStruct((adapter, part), F32),
            jax.ShapeDtypeStruct((1, part), F32),
        ),
        in_specs=[pl.BlockSpec(memory_space=pltpu.SMEM)] + [anywhere] * 7,
        out_specs=(anywhere, in_vmem, in_vmem, in_vmem),
        scratch_shapes=[
            pltpu.VMEM(in_table.shape, BF16),
            pltpu.VMEM(sent_table.shape, BF16),
            pltpu.VMEM(exps.shape, jnp.int32),
            pltpu.VMEM((1, features), F32),
            whole, whole, whole, whole, whole,
            pltpu.VMEM((RC, features // PIECES), BF16),
            pltpu.VMEM((features, adapter), BF16),
            pltpu.VMEM((adapter, features), BF16),
            pltpu.VMEM((adapter, features), BF16),
            pltpu.VMEM((features, adapter), BF16),
            pltpu.VMEM(grouped + (part,), BF16),
            pltpu.VMEM(grouped + (part,), BF16),
            pltpu.VMEM(grouped + (adapter,), BF16),
            pltpu.VMEM(grouped + (adapter,), BF16),
            pltpu.VMEM((tokens, adapter), F32),
            pltpu.VMEM((tokens, BLOCK), F32),
            dma((6,)), dma((chunks, PIECES)), dma((chunks, PIECES)), dma((2,)),
            dma((4, replicas)), dma((4, GROUPS, replicas)), dma,
        ],
        compiler_params=pltpu.CompilerParams(
            collective_id=0, has_side_effects=True, vmem_limit_bytes=60 * 2**20
        ),
        cost_estimate=pl.CostEstimate(
            flops=12 * tokens * features * adapter, bytes_accessed=24 * 2**20, transcendentals=0
        ),
        name="relay",
    )(ids, exps, in_table, sent_table, cotangent, w_down, w_up, gain)


def finish_kernel(reb_hbm, pdown, pup, pgain, out_reb, grad_down, grad_up, gain_grad, sems):
    pieces = sems.shape[0]
    step = reb_hbm.shape[0] // pieces
    copies = [
        pltpu.make_async_copy(
            reb_hbm.at[pl.ds(i * step, step)], out_reb.at[pl.ds(i * step, step)], sems.at[i]
        )
        for i in range(pieces)
    ]
    for copy in copies:
        copy.start()
    grad_down[...] = pdown[...].T
    grad_up[...] = pup[...]
    gain_grad[...] = pgain[...]
    for copy in copies:
        copy.wait()


def finish(rebuilt, pdown, pup, pgain):
    anywhere = pl.BlockSpec(memory_space=pl.ANY)
    in_vmem = pl.BlockSpec(memory_space=pltpu.VMEM)
    return pl.pallas_call(
        finish_kernel,
        out_shape=(
            jax.ShapeDtypeStruct(rebuilt.shape, BF16),
            jax.ShapeDtypeStruct(pdown.shape[::-1], F32),
            jax.ShapeDtypeStruct(pup.shape, F32),
            jax.ShapeDtypeStruct(pgain.shape, F32),
        ),
        in_specs=[anywhere, in_vmem, in_vmem, in_vmem],
        out_specs=(anywhere, in_vmem, in_vmem, in_vmem),
        scratch_shapes=[pltpu.SemaphoreType.DMA((6,))],
        compiler_params=pltpu.CompilerParams(vmem_limit_bytes=60 * 2**20),
        name="finish",
    )(rebuilt, pdown, pup, pgain)


def solution(mesh):
    sections, replicas = mesh.shape["section"], mesh.shape["dp"]

    def on_device(in_bases, sent_bases, sample_ids, exponents, cotangent, w_down, w_up, norm_gain):
        micro, rows, features = cotangent.shape[1:]
        flat = (-1, features)
        rebuilt, pdown, pup, pgain = relay_call(
            sections, replicas, rows, sample_ids, exponents[0].reshape(micro * rows, -1),
            in_bases[0, 0].reshape(flat), sent_bases[0, 0].reshape(flat),
            cotangent[0].reshape(flat), w_down[0], w_up[0], norm_gain,
        )
        rebuilt, grad_down, grad_up, gain_grad = finish(rebuilt, pdown, pup, pgain)
        return (
            rebuilt.reshape(1, 1, micro, rows, features),
            grad_down[None],
            grad_up[None],
            gain_grad,
        )

    return jax.shard_map(
        on_device,
        mesh=mesh,
        in_specs=(
            P("section", "dp", None, None, None),
            P("section", "dp", None, None, None),
            P("dp", None),
            P("dp", None, None, None),
            P("dp", None, None, None),
            P("section", None, None),
            P("section", None, None),
            P("section", None),
        ),
        out_specs=(
            P("section", "dp", None, None, None),
            P("section", "dp", None),
            P("section", None, "dp"),
            P("section", "dp"),
        ),
        check_vma=False,
    )
```

time: 279 us -> 318 us (1.14)
  Pallas kernels: 257 us -> 318 us
  local copies, waits for them, and re-layouts: 19 us -> 0 us
    pallas_call x2, Pallas kernels: 257 us -> 318 us  [the longest x1 218 us: relay_call(): pl.pallas_call(functools.partial(relay_kernel, sections, replicas, slab),...]
    unnamed x20 -> x0, local copies, waits for them, and re-layouts: 17.2 us -> none
where the time goes in v2:
time: 318 us
  Pallas kernels  318 us (100%)
    pallas_call x1, Pallas kernels, relay_call(): pl.pallas_call(functools.partial(relay_kernel, sections, replicas, slab),...  218 us
    pallas_call x1, Pallas kernels, finish(): pl.pallas_call(finish_kernel, out_shape=(jax.ShapeDtypeStruct(rebuilt.sha...  99.3 us

profile of v2, /device:TPU:0, one launch (start us, length us, event | category | flops | bytes accessed | tf_op | source)
XLA Modules:
  0.0 318.3 jit_solution(5750738487691015478)
XLA Ops:
  0.6 218.3 %relay.1 = (bf16[192,8192]{1,0:T(8,128)(2,1)}, f32[256,1024]{1,0:T(8,128)}, f32[256,1024]{1,0:T(8,128)}, f32[1,1024]{1,0:T(1,128)}) custom-call(s32[1,8]{1,0:T(1,128)} %ids.1, s32[192,64]{1,0:T(8,128)} %bitcast.14, bf16[240,8192]{1,0:T(8,128)(2,1)} %bitcast.11, bf16[240,8192]{1,0:T(8,128)(2,1)} %bitcast.12, bf16[192,8192]{1,0:T(8,128)(2,1)} %bitcast.13, ...), custom_call_target="tpu_custom_call" | custom-call | flops 4831838208 | bytes 25165824 | tf_op jit(solution)/shard_map/relay/pallas_call | solution.py:419
  218.9 99.3 %finish.1 = (bf16[192,8192]{1,0:T(8,128)(2,1)}, f32[1024,256]{1,0:T(8,128)}, f32[256,1024]{1,0:T(8,128)}, f32[1,1024]{1,0:T(1,128)}) custom-call(bf16[192,8192]{1,0:T(8,128)(2,1)} %get-tuple-element.12.reb_hbm, f32[256,1024]{1,0:T(8,128)} %get-tuple-element.13.pdown, f32[256,1024]{1,0:T(8,128)} %get-tuple-element.14.pup, f32[1,1024]{1,0:T(1,128)} %get-tuple-element.15.pgain), custom_call_target="tpu_custom_call" | custom-call | tf_op jit(solution)/shard_map/finish/pallas_call | solution.py:480

commit v3 on v2

--- a/solution.py
+++ b/solution.py
@@ -13,6 +13,7 @@
 RC = 16
 PIECES = 2
 UNIT = 2
+LAG_TOP, LAG_BOTTOM = 8, 3
 GROUPS = 3
 MESH = pl.DeviceIdType.MESH
 F32 = jnp.float32
@@ -190,17 +191,16 @@
 
         lax.fori_loop(0, replicas - 1, to_peer, 0)
 
-    def share_forward():
+    def share_whole(kinds, buffer):
         def one(group, _):
-            share(0, base, group * per_group, per_group)
+            share(kinds, buffer, group * per_group, per_group)
             return 0
 
         lax.fori_loop(0, GROUPS, one, 0)
 
     own = pl.ds(pl.multiple_of(b * part, part), part)
     early = s < sections // 4
-    pause_mid, pause_end = s < sections // 2, s >= sections * 3 // 4
-    within = jnp.logical_not(jnp.logical_or(pause_mid, pause_end))
+    pause_mid, pause_end = s < sections // 2, s >= sections // 2
 
     def forward(chunk):
         rows = rows_of(chunk)
@@ -257,7 +257,7 @@
         pltpu.make_async_copy(base.at[rows, :], reb_hbm.at[rows, :], out_sem).start()
         rb_all[group, b, spot, :] = base[rows, own]
 
-        @pl.when(jnp.logical_and(within, chunk % UNIT == UNIT - 1))
+        @pl.when(jnp.logical_and(jnp.logical_not(pause_mid), chunk % UNIT == UNIT - 1))
         def _():
             share(0, base, chunk - (UNIT - 1), UNIT)
 
@@ -298,7 +298,7 @@
 
         go_all[group, b, spot, :] = go[rows, own]
 
-        @pl.when(chunk % UNIT == UNIT - 1)
+        @pl.when(jnp.logical_and(jnp.logical_not(pause_end), chunk % UNIT == UNIT - 1))
         def _():
             share(2, go, chunk - (UNIT - 1), UNIT)
 
@@ -330,31 +330,32 @@
 
     pdown[...] = jnp.zeros_like(pdown)
     pup[...] = jnp.zeros_like(pup)
-    turn_tick = jnp.where(early, chunks - 1 + s, 0)
+    turn_tick = jnp.where(early, chunks - 1, 0)
+    lag = (sections - 1 - s) * LAG_TOP // LAG_BOTTOM
     spare = s < sections // 2
 
     def tick(t, _):
-        f_chunk = t - s
-        b_chunk = t - (2 * sections - 2 - s)
+        f_chunk = t
+        b_chunk = t - lag
 
         @pl.when(jnp.logical_and(t == turn_tick, jnp.logical_not(early)))
         def _():
             loads[4].wait()
             transpose_weights()
 
-        @pl.when(jnp.logical_and(f_chunk >= 0, f_chunk < chunks))
+        @pl.when(f_chunk < chunks)
         def _():
             forward(f_chunk)
 
         @pl.when(jnp.logical_and(pause_mid, f_chunk == chunks - 1))
         def _():
-            share_forward()
+            share_whole(0, base)
 
         @pl.when(jnp.logical_and(t == turn_tick, early))
         def _():
             transpose_weights()
 
-        @pl.when(jnp.logical_and(b_chunk >= 0, b_chunk < chunks))
+        @pl.when(b_chunk >= 0)
         def _():
             backward(b_chunk)
 
@@ -365,11 +366,11 @@
 
         return 0
 
-    lax.fori_loop(0, 2 * sections - 2 + chunks, tick, 0)
+    lax.fori_loop(0, lag + chunks, tick, 0)
 
     @pl.when(pause_end)
     def _():
-        share_forward()
+        share_whole(2, go)
 
     def remaining(group, _):
         collect(group)
@@ -456,38 +457,31 @@
     )(ids, exps, in_table, sent_table, cotangent, w_down, w_up, gain)
 
 
-def finish_kernel(reb_hbm, pdown, pup, pgain, out_reb, grad_down, grad_up, gain_grad, sems):
-    pieces = sems.shape[0]
-    step = reb_hbm.shape[0] // pieces
-    copies = [
-        pltpu.make_async_copy(
-            reb_hbm.at[pl.ds(i * step, step)], out_reb.at[pl.ds(i * step, step)], sems.at[i]
-        )
-        for i in range(pieces)
-    ]
-    for copy in copies:
-        copy.start()
+def finish_kernel(reb, pdown, pup, pgain, out_reb, grad_down, grad_up, gain_grad):
+    out_reb[...] = reb[...]
     grad_down[...] = pdown[...].T
     grad_up[...] = pup[...]
     gain_grad[...] = pgain[...]
-    for copy in copies:
-        copy.wait()
 
 
 def finish(rebuilt, pdown, pup, pgain):
-    anywhere = pl.BlockSpec(memory_space=pl.ANY)
-    in_vmem = pl.BlockSpec(memory_space=pltpu.VMEM)
+    steps = 4
+    (tokens, features), (adapter, part) = rebuilt.shape, pdown.shape
+    block = pl.BlockSpec((tokens // steps, features), lambda i: (i, 0))
+    across = pl.BlockSpec((adapter, part // steps), lambda i: (0, i))
+    down = pl.BlockSpec((part // steps, adapter), lambda i: (i, 0))
+    gains = pl.BlockSpec((1, part // steps), lambda i: (0, i))
     return pl.pallas_call(
         finish_kernel,
         out_shape=(
             jax.ShapeDtypeStruct(rebuilt.shape, BF16),
-            jax.ShapeDtypeStruct(pdown.shape[::-1], F32),
+            jax.ShapeDtypeStruct((part, adapter), F32),
             jax.ShapeDtypeStruct(pup.shape, F32),
             jax.ShapeDtypeStruct(pgain.shape, F32),
         ),
-        in_specs=[anywhere, in_vmem, in_vmem, in_vmem],
-        out_specs=(anywhere, in_vmem, in_vmem, in_vmem),
-        scratch_shapes=[pltpu.SemaphoreType.DMA((6,))],
+        grid=(steps,),
+        in_specs=[block, across, across, gains],
+        out_specs=(block, down, across, gains),
         compiler_params=pltpu.CompilerParams(vmem_limit_bytes=60 * 2**20),
         name="finish",
     )(rebuilt, pdown, pup, pgain)

time: 318 us -> 200 us (0.63)
  Pallas kernels: 318 us -> 199 us
    pallas_call x1, Pallas kernels: 99.3 us -> 5.26 us  [finish(): pl.pallas_call(finish_kernel, out_shape=(jax.ShapeDtypeStruct(rebuilt.sha...]
    pallas_call x1, Pallas kernels: 218 us -> 194 us  [relay_call(): pl.pallas_call(functools.partial(relay_kernel, sections, replicas, slab),...]
where the time goes in v3:
time: 200 us; the launch traced here: 199 us
  Pallas kernels  199 us (100%)
    pallas_call x1, Pallas kernels, relay_call(): pl.pallas_call(functools.partial(relay_kernel, sections, replicas, slab),...  194 us
    pallas_call x1, Pallas kernels, finish(): pl.pallas_call(finish_kernel, out_shape=(jax.ShapeDtypeStruct(rebuilt.sha...  5.26 us

profile of v3, /device:TPU:0, one launch (start us, length us, event | category | flops | bytes accessed | tf_op | source)
XLA Modules:
  0.0 199.4 jit_solution(15632453548395234650)
XLA Ops:
  0.6 193.5 %relay.1 = (bf16[192,8192]{1,0:T(8,128)(2,1)}, f32[256,1024]{1,0:T(8,128)}, f32[256,1024]{1,0:T(8,128)}, f32[1,1024]{1,0:T(1,128)}) custom-call(s32[1,8]{1,0:T(1,128)} %ids.1, s32[192,64]{1,0:T(8,128)} %bitcast.14, bf16[240,8192]{1,0:T(8,128)(2,1)} %bitcast.11, bf16[240,8192]{1,0:T(8,128)(2,1)} %bitcast.12, bf16[192,8192]{1,0:T(8,128)(2,1)} %bitcast.13, ...), custom_call_target="tpu_custom_call" | custom-call | flops 4831838208 | bytes 25165824 | tf_op jit(solution)/shard_map/relay/pallas_call | solution.py:420
  194.1 5.3 %finish.1 = (bf16[192,8192]{1,0:T(8,128)(2,1)}, f32[1024,256]{1,0:T(8,128)}, f32[256,1024]{1,0:T(8,128)}, f32[1,1024]{1,0:T(1,128)}) custom-call(bf16[192,8192]{1,0:T(8,128)(2,1)} %get-tuple-element.12.reb, f32[256,1024]{1,0:T(8,128)} %get-tuple-element.13.pdown, f32[256,1024]{1,0:T(8,128)} %get-tuple-element.14.pup, f32[1,1024]{1,0:T(1,128)} %get-tuple-element.15.pgain), custom_call_target="tpu_custom_call" | custom-call | tf_op jit(solution)/shard_map/finish/pallas_call | solution.py:474

commit v4 on v3

--- a/solution.py
+++ b/solution.py
@@ -12,7 +12,7 @@
 EPSILON = 1e-05
 RC = 16
 PIECES = 2
-UNIT = 2
+UNIT = 1
 LAG_TOP, LAG_BOTTOM = 8, 3
 GROUPS = 3
 MESH = pl.DeviceIdType.MESH
@@ -465,7 +465,7 @@
 
 
 def finish(rebuilt, pdown, pup, pgain):
-    steps = 4
+    steps = 2
     (tokens, features), (adapter, part) = rebuilt.shape, pdown.shape
     block = pl.BlockSpec((tokens // steps, features), lambda i: (i, 0))
     across = pl.BlockSpec((adapter, part // steps), lambda i: (0, i))

time: 200 us -> 198 us (0.990)
  Pallas kernels: 199 us -> 195 us
    pallas_call x1, Pallas kernels: 194 us -> 191 us  [relay_call(): pl.pallas_call(functools.partial(relay_kernel, sections, replicas, slab),...]
where the time goes in v4:
time: 198 us; the launch traced here: 196 us
  Pallas kernels  195 us (98%)
    pallas_call x1, Pallas kernels, relay_call(): pl.pallas_call(functools.partial(relay_kernel, sections, replicas, slab),...  191 us
    pallas_call x1, Pallas kernels, finish(): pl.pallas_call(finish_kernel, out_shape=(jax.ShapeDtypeStruct(rebuilt.sha...  4.28 us

profile of v4, /device:TPU:0, one launch (start us, length us, event | category | flops | bytes accessed | tf_op | source)
XLA Modules:
  0.0 196.0 jit_solution(14353095361940011278)
XLA Ops:
  0.6 191.0 %relay.1 = (bf16[192,8192]{1,0:T(8,128)(2,1)}, f32[256,1024]{1,0:T(8,128)}, f32[256,1024]{1,0:T(8,128)}, f32[1,1024]{1,0:T(1,128)}) custom-call(s32[1,8]{1,0:T(1,128)} %ids.1, s32[192,64]{1,0:T(8,128)} %bitcast.14, bf16[240,8192]{1,0:T(8,128)(2,1)} %bitcast.11, bf16[240,8192]{1,0:T(8,128)(2,1)} %bitcast.12, bf16[192,8192]{1,0:T(8,128)(2,1)} %bitcast.13, ...), custom_call_target="tpu_custom_call" | custom-call | flops 4831838208 | bytes 25165824 | tf_op jit(solution)/shard_map/relay/pallas_call | solution.py:420
  191.7 4.3 %finish.1 = (bf16[192,8192]{1,0:T(8,128)(2,1)}, f32[1024,256]{1,0:T(8,128)}, f32[256,1024]{1,0:T(8,128)}, f32[1,1024]{1,0:T(1,128)}) custom-call(bf16[192,8192]{1,0:T(8,128)(2,1)} %get-tuple-element.12.reb, f32[256,1024]{1,0:T(8,128)} %get-tuple-element.13.pdown, f32[256,1024]{1,0:T(8,128)} %get-tuple-element.14.pup, f32[1,1024]{1,0:T(1,128)} %get-tuple-element.15.pgain), custom_call_target="tpu_custom_call" | custom-call | tf_op jit(solution)/shard_map/finish/pallas_call | solution.py:474

commit v5 on v4

--- a/solution.py
+++ b/solution.py
@@ -14,6 +14,7 @@
 PIECES = 2
 UNIT = 1
 LAG_TOP, LAG_BOTTOM = 8, 3
+PROMPT = 2
 GROUPS = 3
 MESH = pl.DeviceIdType.MESH
 F32 = jnp.float32
@@ -191,16 +192,17 @@
 
         lax.fori_loop(0, replicas - 1, to_peer, 0)
 
-    def share_whole(kinds, buffer):
+    def share_whole(kinds, buffer, start):
         def one(group, _):
             share(kinds, buffer, group * per_group, per_group)
             return 0
 
-        lax.fori_loop(0, GROUPS, one, 0)
+        lax.fori_loop(start, GROUPS, one, 0)
 
     own = pl.ds(pl.multiple_of(b * part, part), part)
     early = s < sections // 4
     pause_mid, pause_end = s < sections // 2, s >= sections // 2
+    prompt = jnp.where(s >= sections * 3 // 4, PROMPT, GROUPS)
 
     def forward(chunk):
         rows = rows_of(chunk)
@@ -257,7 +259,7 @@
         pltpu.make_async_copy(base.at[rows, :], reb_hbm.at[rows, :], out_sem).start()
         rb_all[group, b, spot, :] = base[rows, own]
 
-        @pl.when(jnp.logical_and(jnp.logical_not(pause_mid), chunk % UNIT == UNIT - 1))
+        @pl.when(pause_end & (chunk < prompt * per_group) & (chunk % UNIT == UNIT - 1))
         def _():
             share(0, base, chunk - (UNIT - 1), UNIT)
 
@@ -349,7 +351,7 @@
 
         @pl.when(jnp.logical_and(pause_mid, f_chunk == chunks - 1))
         def _():
-            share_whole(0, base)
+            share_whole(0, base, 0)
 
         @pl.when(jnp.logical_and(t == turn_tick, early))
         def _():
@@ -370,7 +372,8 @@
 
     @pl.when(pause_end)
     def _():
-        share_whole(2, go)
+        share_whole(0, base, prompt)
+        share_whole(2, go, 0)
 
     def remaining(group, _):
         collect(group)

time: 198 us -> 198 us (level)
  no operation moved by 1% of the time
where the time goes in v5:
time: 198 us; the launch traced here: 196 us
  Pallas kernels  195 us (98%)
    pallas_call x1, Pallas kernels, relay_call(): pl.pallas_call(functools.partial(relay_kernel, sections, replicas, slab),...  191 us
    pallas_call x1, Pallas kernels, finish(): pl.pallas_call(finish_kernel, out_shape=(jax.ShapeDtypeStruct(rebuilt.sha...  4.28 us

profile of v5, /device:TPU:0, one launch (start us, length us, event | category | flops | bytes accessed | tf_op | source)
XLA Modules:
  0.0 195.6 jit_solution(12473924047937115171)
XLA Ops:
  0.6 190.7 %relay.1 = (bf16[192,8192]{1,0:T(8,128)(2,1)}, f32[256,1024]{1,0:T(8,128)}, f32[256,1024]{1,0:T(8,128)}, f32[1,1024]{1,0:T(1,128)}) custom-call(s32[1,8]{1,0:T(1,128)} %ids.1, s32[192,64]{1,0:T(8,128)} %bitcast.14, bf16[240,8192]{1,0:T(8,128)(2,1)} %bitcast.11, bf16[240,8192]{1,0:T(8,128)(2,1)} %bitcast.12, bf16[192,8192]{1,0:T(8,128)(2,1)} %bitcast.13, ...), custom_call_target="tpu_custom_call" | custom-call | flops 4831838208 | bytes 25165824 | tf_op jit(solution)/shard_map/relay/pallas_call | solution.py:423
  191.4 4.3 %finish.1 = (bf16[192,8192]{1,0:T(8,128)(2,1)}, f32[1024,256]{1,0:T(8,128)}, f32[256,1024]{1,0:T(8,128)}, f32[1,1024]{1,0:T(1,128)}) custom-call(bf16[192,8192]{1,0:T(8,128)(2,1)} %get-tuple-element.12.reb, f32[256,1024]{1,0:T(8,128)} %get-tuple-element.13.pdown, f32[256,1024]{1,0:T(8,128)} %get-tuple-element.14.pup, f32[1,1024]{1,0:T(1,128)} %get-tuple-element.15.pgain), custom_call_target="tpu_custom_call" | custom-call | tf_op jit(solution)/shard_map/finish/pallas_call | solution.py:477

commit v6 on v4

--- a/solution.py
+++ b/solution.py
@@ -257,9 +257,9 @@
         pltpu.make_async_copy(base.at[rows, :], reb_hbm.at[rows, :], out_sem).start()
         rb_all[group, b, spot, :] = base[rows, own]
 
-        @pl.when(jnp.logical_and(jnp.logical_not(pause_mid), chunk % UNIT == UNIT - 1))
-        def _():
-            share(0, base, chunk - (UNIT - 1), UNIT)
+        @pl.when(jnp.logical_and(jnp.logical_not(pause_mid), chunk % 2 == 1))
+        def _():
+            share(0, base, chunk - 1, 2)
 
     def backward(chunk):
         rows = rows_of(chunk)

time: 198 us -> 198 us (level)
  no operation moved by 1% of the time
where the time goes in v6:
time: 198 us; the launch traced here: 196 us
  Pallas kernels  195 us (98%)
    pallas_call x1, Pallas kernels, relay_call(): pl.pallas_call(functools.partial(relay_kernel, sections, replicas, slab),...  191 us
    pallas_call x1, Pallas kernels, finish(): pl.pallas_call(finish_kernel, out_shape=(jax.ShapeDtypeStruct(rebuilt.sha...  4.28 us

profile of v6, /device:TPU:0, one launch (start us, length us, event | category | flops | bytes accessed | tf_op | source)
XLA Modules:
  0.0 195.8 jit_solution(11731545854225592612)
XLA Ops:
  0.6 190.9 %relay.1 = (bf16[192,8192]{1,0:T(8,128)(2,1)}, f32[256,1024]{1,0:T(8,128)}, f32[256,1024]{1,0:T(8,128)}, f32[1,1024]{1,0:T(1,128)}) custom-call(s32[1,8]{1,0:T(1,128)} %ids.1, s32[192,64]{1,0:T(8,128)} %bitcast.14, bf16[240,8192]{1,0:T(8,128)(2,1)} %bitcast.11, bf16[240,8192]{1,0:T(8,128)(2,1)} %bitcast.12, bf16[192,8192]{1,0:T(8,128)(2,1)} %bitcast.13, ...), custom_call_target="tpu_custom_call" | custom-call | flops 4831838208 | bytes 25165824 | tf_op jit(solution)/shard_map/relay/pallas_call | solution.py:420
  191.5 4.3 %finish.1 = (bf16[192,8192]{1,0:T(8,128)(2,1)}, f32[1024,256]{1,0:T(8,128)}, f32[256,1024]{1,0:T(8,128)}, f32[1,1024]{1,0:T(1,128)}) custom-call(bf16[192,8192]{1,0:T(8,128)(2,1)} %get-tuple-element.12.reb, f32[256,1024]{1,0:T(8,128)} %get-tuple-element.13.pdown, f32[256,1024]{1,0:T(8,128)} %get-tuple-element.14.pup, f32[1,1024]{1,0:T(1,128)} %get-tuple-element.15.pgain), custom_call_target="tpu_custom_call" | custom-call | tf_op jit(solution)/shard_map/finish/pallas_call | solution.py:474
